TPU v7x, 256 devices: a whole 4x4x8 slice. The times are simulated.
256 devices in a mesh: own: 64 (over z, y, core), rep: 4 (over x).
Axes of the slice: x: 4, y: 4, z: 8, core: 2. Of those that a mesh axis runs over, the one named last changes fastest.
Arguments:
- h_in: bfloat16 [32768, 1024], P('own'), may hold values from -16 to 16
- send_rows: int32 [64, 4, 64, 32], P('own', 'rep'), may hold values from 0 to 511
- counts: int32 [64, 4, 64], P('own', 'rep'), may hold values from 1 to 32, as said below
- seed_rows: int32 [64, 4, 256], P('own', 'rep'), may hold values from 0 to 511
- nbr_slot: int32 [64, 4, 256, 8], P('own', 'rep'), may hold values from 0 to 2047, as said below
- degree: int32 [64, 4, 256], P('own', 'rep'), may hold values from 1 to 8
- g_out: bfloat16 [64, 4, 256, 1024], P('own', 'rep'), may hold values from -6 to 6
- weights: bfloat16 [2048, 1024], replicated, may hold values from -0.125 to 0.125
- master: float32 [2048, 1024], P(('own', 'rep')), may hold values from -0.125 to 0.125
- moment: float32 [2048, 1024], P(('own', 'rep')), may hold values from -0.002 to 0.002
- second: float32 [2048, 1024], P(('own', 'rep')), may hold values from 1e-09 to 1e-07
Outputs:
- h_out: bfloat16 [64, 4, 256, 1024], P('own', 'rep')
- grad_in: float32 [32768, 1024], P('own')
- weights_new: bfloat16 [2048, 1024], replicated
- master_new: float32 [2048, 1024], P(('own', 'rep'))
- moment_new: float32 [2048, 1024], P(('own', 'rep'))
- second_new: float32 [2048, 1024], P(('own', 'rep'))
Inputs may be any that keep to these rules, and one draw needn't show every extreme that they name: counts[o, r, p] is the used slots of the block from owner o to device (p, r); for each r one destination p gets 32 from every owner. nbr_slot[p, r, s, f] = o * 32 + j names slot j of the block from owner o to device (p, r), with j < counts[o, r, p].
All inputs are finite; a program needn't handle non-finite values.
Results may differ from a plain program's by a relative error of at most 0.004.
Values may be sent and summed in bfloat16 or wider, within the bound.
No kernel may reach another device: no remote copies, remote signals or barrier semaphores. Data moves between devices by JAX's collectives and lax.ppermute only.
A program may use at most 128 MiB of HBM per device.

v0:
```python
import jax
import jax.numpy as jnp
from jax import lax
from jax.sharding import PartitionSpec as P

ADAM_STEP = 10


beta_first = 0.9
beta_second = 0.999
learning = 0.001
epsilon = 1e-08


def tally_slots(slots, degree, width):
    positions = jnp.arange(width, dtype=jnp.int32)
    total = jnp.zeros((slots.shape[0], width), jnp.float32)
    for column in range(slots.shape[1]):
        matches = (slots[:, column][:, None] == positions[None, :]) & (column < degree)[:, None]
        total = total + matches.astype(jnp.float32)
    return total.astype(jnp.bfloat16)


def device_pass(received, self_rows, slots, degree, cotangent, weights):
    tallies = tally_slots(slots, degree, received.shape[0])
    divisor = degree.astype(jnp.float32)[:, None]
    gathered = (jnp.dot(tallies, received, preferred_element_type=jnp.float32) / divisor).astype(
        jnp.bfloat16
    )
    joined = jnp.concatenate([self_rows, gathered], axis=1)
    before = jnp.dot(joined, weights, preferred_element_type=jnp.float32)
    logistic = jax.nn.sigmoid(before)
    h_out = (before * logistic).astype(jnp.bfloat16)
    d_before = (
        cotangent.astype(jnp.float32) * logistic * (1.0 + before * (1.0 - logistic))
    ).astype(jnp.bfloat16)
    backward = lax.dot_general(
        d_before, weights, (((1,), (1,)), ((), ())), preferred_element_type=jnp.float32
    )
    hidden = weights.shape[1]
    d_self = backward[:, :hidden]
    d_scaled = (backward[:, hidden:] / divisor).astype(jnp.bfloat16)
    d_received = lax.dot_general(
        tallies, d_scaled, (((0,), (0,)), ((), ())), preferred_element_type=jnp.float32
    ).astype(jnp.bfloat16)
    return (h_out, joined, d_before, d_self, d_received)


def adam_update(grad_sum, master, moment, second, seed_total):
    grad = grad_sum / seed_total
    moment_new = beta_first * moment + (1.0 - beta_first) * grad
    second_new = beta_second * second + (1.0 - beta_second) * grad * grad
    corrected_m = moment_new / (1.0 - beta_first**ADAM_STEP)
    corrected_v = second_new / (1.0 - beta_second**ADAM_STEP)
    master_new = master - learning * corrected_m / (jnp.sqrt(corrected_v) + epsilon)
    return (master_new, moment_new, second_new)


def per_device(
    h_in, send_rows, counts, seed_rows, nbr_slot, degree, g_out, weights, master, moment, second
):
    peer_count = send_rows.shape[2]
    block_rows = send_rows.shape[3]
    hidden = h_in.shape[1]
    send_ids = send_rows.reshape(peer_count, block_rows)
    filled = jnp.arange(block_rows, dtype=jnp.int32)[None, :] < counts.reshape(peer_count)[:, None]
    outgoing = jnp.where(filled[:, :, None], h_in[send_ids], jnp.zeros((), jnp.bfloat16))
    received = lax.all_to_all(outgoing, "own", split_axis=0, concat_axis=0, tiled=True)
    seed_ids = seed_rows.reshape(-1)
    seed_count = seed_ids.shape[0]
    self_rows = h_in[seed_ids]
    h_out, joined, d_before, d_self, d_received = device_pass(
        received.reshape(peer_count * block_rows, hidden),
        self_rows,
        nbr_slot.reshape(seed_count, -1),
        degree.reshape(seed_count),
        g_out.reshape(seed_count, hidden),
        weights,
    )
    returned = lax.all_to_all(
        d_received.reshape(peer_count, block_rows, hidden),
        "own",
        split_axis=0,
        concat_axis=0,
        tiled=True,
    )
    kept_grads = jnp.where(filled[:, :, None], returned.astype(jnp.float32), jnp.float32(0.0))
    owner_grad = (
        jnp.zeros(h_in.shape, jnp.float32)
        .at[send_ids.reshape(-1)]
        .add(kept_grads.reshape(-1, hidden))
    )
    owner_grad = owner_grad.at[seed_ids].add(d_self)
    grad_in = lax.psum(owner_grad, "rep")
    grad_sum = lax.psum_scatter(
        lax.dot_general(
            joined, d_before, (((0,), (0,)), ((), ())), preferred_element_type=jnp.float32
        ),
        ("own", "rep"),
        scatter_dimension=0,
        tiled=True,
    )
    seed_total = float(seed_count * lax.axis_size("own") * lax.axis_size("rep"))
    master_new, moment_new, second_new = adam_update(grad_sum, master, moment, second, seed_total)
    rounded = master_new.astype(jnp.bfloat16)
    weights_new = lax.all_gather(rounded, ("own", "rep"), axis=0, tiled=True)
    return (h_out.reshape(g_out.shape), grad_in, weights_new, master_new, moment_new, second_new)


def solution(mesh):
    return jax.shard_map(
        per_device,
        mesh=mesh,
        in_specs=(
            P("own", None),
            P("own", "rep", None, None),
            P("own", "rep", None),
            P("own", "rep", None),
            P("own", "rep", None, None),
            P("own", "rep", None),
            P("own", "rep", None, None),
            P(),
            P(("own", "rep"), None),
            P(("own", "rep"), None),
            P(("own", "rep"), None),
        ),
        out_specs=(
            P("own", "rep", None, None),
            P("own", None),
            P(),
            P(("own", "rep"), None),
            P(("own", "rep"), None),
            P(("own", "rep"), None),
        ),
        check_vma=False,
    )
```

profile of v0, /device:TPU:1, one launch (start us, length us, event | category | flops | bytes accessed | tf_op | source)
XLA Modules:
  0.0 1569.2 jit_solution(13289458655362638951)
XLA Ops:
  8.0 0.0 copy-start
  8.0 0.8 iota_compare_fusion.8
  8.8 0.7 compare_select_fusion.1
  9.6 0.1 copy.17
  9.6 0.1 reshape.225
  9.7 0.0 copy-done
  9.7 9.6 gather_fusion.1
  19.3 3.8 broadcast_select_fusion
  23.2 0.0 copy-start.11
  23.2 0.0 copy-start.12
  23.2 13.5 all-to-all-start
  36.7 0.0 reduce-scatter.2.cloned.1.call-start
  36.7 0.0 copy-done.11
  36.7 0.0 copy-done.12
  36.8 0.0 copy-start.10
  36.8 1.2 gather_fusion
  38.0 0.0 copy-done.10
  38.0 93.1 %all-to-all-done = bf16[64,32,1024]{2,1,0:T(8,128)(2,1)} async-done(((bf16[64,32,1024]{2,1,0:T(8,128)(2,1)}), bf16[64,32,1024]{2,1,0:T(8,128)(2,1)}, u32[]{:S(2)}, u32[]{:S(2)}) %all-to-all-start) | async-done | bytes 4194336 | tf_op jit(solution)/shard_map/all_to_all | solution.py:68
  131.1 0.0 copy-start.13
  131.1 6.4 fusion.8
  137.5 0.0 copy-done.13
  137.5 0.0 copy-start.5
  137.5 1.3 fusion.17
  138.8 0.0 copy-done.5
  138.8 0.0 copy-start.2
  138.8 4.7 fusion.16
  143.5 0.0 reduce-scatter.2.cloned.1.call-update
  143.5 0.0 copy-done.2
  143.5 3.6 fusion.24
  147.2 0.0 copy-start.4
  147.2 6.5 convolution_convert_fusion
  153.7 0.0 copy-done.4
  153.7 0.0 copy-start.7
  153.7 0.0 copy-start.8
  153.7 0.0 copy-start.9
  153.7 0.0 copy-start.6
  153.7 7.5 all-to-all-start.1
  161.3 0.0 all-gather.2.cloned.1.call-start
  161.3 1269.4 %reduce-scatter.2.cloned.1.call-done = f32[8,1024]{1,0:T(8,128)} async-done(((f32[2048,1024]{1,0:T(8,128)}), f32[8,1024]{1,0:T(8,128)}) %reduce-scatter.2.cloned.1.call-update) | async-done | bytes 32784 | tf_op jit(solution)/shard_map/reduce_scatter | solution.py:95
  1430.7 0.0 copy-done.7
  1430.7 0.0 copy-done.8
  1430.7 0.0 copy-done.9
  1430.7 1.4 fusion.26
  1432.1 0.0 all-gather.2.cloned.1.call-update
  1432.1 0.0 all-reduce.2.cloned.1.call-start
  1432.2 0.0 copy-done.6
  1432.2 0.1 copy.18
  1432.3 0.1 reshape_reshape.3
  1432.4 0.0 all-to-all-done.1
  1432.4 5.2 convert_select_fusion
  1437.6 19.5 %scatter_custom_fusion = f32[512,1024]{1,0:T(8,128)S(1)} fusion(s32[2048]{0:T(1024)S(1)} %bitcast.39, f32[2048,1024]{1,0:T(8,128)} %bitcast.36, f32[]{:T(128)} %constant.12.clone.1), kind=kCustom, calls=%fused_computation.34 | custom fusion | flops 2097152 | bytes 2097664 | tf_op jit(solution)/shard_map/scatter-add | solution.py:91
  1457.1 4.2 scatter_custom_fusion.1
  1461.2 0.0 copy-start.1
  1461.3 1.3 copy-done.1
  1462.6 0.0 all-reduce.2.cloned.1.call-update
  1462.6 2.3 fusion.20
  1464.9 91.6 %all-gather.2.cloned.1.call-done = bf16[2048,1024]{1,0:T(8,128)(2,1)} async-done(((bf16[8,1024]{1,0:T(8,128)(2,1)}), bf16[2048,1024]{1,0:T(8,128)(2,1)}) %all-gather.2.cloned.1.call-update) | async-done | bytes 4194320 | tf_op jit(solution)/shard_map/all_gather | solution.py:106
  1556.5 0.0 all-reduce.2.cloned.1.call-done
  1556.5 0.0 copy-start.3
  1556.5 3.3 copy.22
  1559.8 0.0 copy-done.3
  1559.8 2.0 copy.23
  (7 shorter events, 0.1 us)
Async XLA Ops:
  8.0 1.7 copy-start
  23.2 13.5 copy-start.11
  23.2 13.6 copy-start.12
  23.2 107.9 %all-to-all-start = ((bf16[64,32,1024]{2,1,0:T(8,128)(2,1)}), bf16[64,32,1024]{2,1,0:T(8,128)(2,1)}, u32[]{:S(2)}, u32[]{:S(2)}) async-start(bf16[64,32,1024]{2,1,0:T(8,128)(2,1)} %broadcast_select_fusion), calls=%async_computation | async-start | bytes 8388608 | tf_op jit(solution)/shard_map/all_to_all | solution.py:68
  36.7 1394.0 %reduce-scatter.2.cloned.1.call-start = ((), (), s32[]{:S(2)}) async-start(), calls=%async_computation.4 | async-start | bytes 8421376 | tf_op jit(solution)/shard_map/reduce_scatter | solution.py:95
  36.8 1.2 copy-start.10
  131.1 6.4 copy-start.13
  137.5 1.3 copy-start.5
  138.8 4.7 copy-start.2
  147.2 6.5 copy-start.4
  153.7 1277.0 %copy-start.7 = (f32[8,1024]{1,0:T(8,128)S(1)}, f32[8,1024]{1,0:T(8,128)}, u32[]{:S(2)}) copy-start(f32[8,1024]{1,0:T(8,128)} %param.19) | copy-start | bytes 98308
  153.7 1277.0 %copy-start.8 = (f32[8,1024]{1,0:T(8,128)S(1)}, f32[8,1024]{1,0:T(8,128)}, u32[]{:S(2)}) copy-start(f32[8,1024]{1,0:T(8,128)} %param.20) | copy-start | bytes 98308
  153.7 1277.0 %copy-start.9 = (f32[8,1024]{1,0:T(8,128)S(1)}, f32[8,1024]{1,0:T(8,128)}, u32[]{:S(2)}) copy-start(f32[8,1024]{1,0:T(8,128)} %param.21) | copy-start | bytes 98308
  153.7 1278.5 %copy-start.6 = (s32[1,1,64,32]{2,3,1,0:T(8,128)S(1)}, s32[1,1,64,32]{2,3,1,0:T(8,128)}, u32[]{:S(2)}) copy-start(s32[1,1,64,32]{2,3,1,0:T(8,128)} %param.12) | copy-start | bytes 24580
  153.7 1278.7 %all-to-all-start.1 = ((bf16[64,32,1024]{2,1,0:T(8,128)(2,1)}), bf16[64,32,1024]{2,1,0:T(8,128)(2,1)}, u32[]{:S(2)}, u32[]{:S(2)}) async-start(bf16[64,32,1024]{2,1,0:T(8,128)(2,1)} %bitcast.37), calls=%async_computation.1 | async-start | bytes 8388608 | tf_op jit(solution)/shard_map/all_to_all | solution.py:80
  161.3 1395.2 %all-gather.2.cloned.1.call-start = ((), (), s32[]{:S(2)}) async-start(), calls=%async_computation.5 | async-start | bytes 4210688 | tf_op jit(solution)/shard_map/all_gather | solution.py:106
  1432.1 124.3 %all-reduce.2.cloned.1.call-start = ((), (), s32[]{:S(2)}) async-start(), calls=%async_computation.3 | async-start | bytes 4194304 | tf_op jit(solution)/shard_map/psum | solution.py:94
  1461.2 1.3 copy-start.1
  1556.5 3.3 copy-start.3
Sparse Core Ops, SparseCore 0:
  143.6 1287.0 reduce-scatter.1
  1434.4 122.0 all-gather.1
Sparse Core Ops, SparseCore 1:
  1462.7 66.8 all-reduce.1
where the time goes:
time: 1570 us
  waiting for transfers between devices  1450 us (92%)
  other arithmetic  38 us (2%)
  matrix products  22.5 us (1%)
  starting transfers between devices  21.1 us (1%)
  local copies, waits for them, and re-layouts  17.8 us (1%)
    reduce_scatter x1, waiting for transfers between devices, per_device(): lax.psum_scatter(lax.dot_general(joined, d_before, (((0,), (0,)), ((), ()...  1270 us
    all_to_all x1, waiting for transfers between devices, per_device(): lax.all_to_all(outgoing, 'own', split_axis=0, concat_axis=0, tiled=True)  93.1 us
    all_gather x1, waiting for transfers between devices, per_device(): weights_new = lax.all_gather(rounded, ('own', 'rep'), axis=0, tiled=True)  91.6 us
  transfers between devices with their start and end apart: 5, of which 3 were waited for; matrix products, arithmetic and copies ran while one was open for 3% of the time, Pallas kernels for 0%

commit v1 on v0

v1 whole, which is shorter than its diff:
```python
import jax
import jax.numpy as jnp
import numpy as np
from jax import lax
from jax.sharding import Mesh
from jax.sharding import PartitionSpec as P

ADAM_STEP = 10

beta_first = 0.9
beta_second = 0.999
learning = 0.001
epsilon = 1e-08

OWN = ("z", "y", "c")
ALL = ("z", "y", "c", "x")
bf16 = jnp.bfloat16
f32 = jnp.float32


def dot(a, b, dims=((1,), (0,))):
    return lax.dot_general(a, b, (dims, ((), ())), preferred_element_type=f32)


def exchange(v, axes):
    return lax.all_to_all(v, axes, split_axis=0, concat_axis=0, tiled=True)


def tally_slots(slots, degree, width):
    positions = jnp.arange(width, dtype=jnp.int32)
    total = jnp.zeros((slots.shape[0], width), f32)
    for column in range(slots.shape[1]):
        matches = (slots[:, column][:, None] == positions[None, :]) & (column < degree)[:, None]
        total = total + matches.astype(f32)
    return total.astype(bf16)


def adam_update(grad_sum, master, moment, second, seed_total):
    grad = grad_sum / seed_total
    moment_new = beta_first * moment + (1.0 - beta_first) * grad
    second_new = beta_second * second + (1.0 - beta_second) * grad * grad
    corrected_m = moment_new / (1.0 - beta_first**ADAM_STEP)
    corrected_v = second_new / (1.0 - beta_second**ADAM_STEP)
    master_new = master - learning * corrected_m / (jnp.sqrt(corrected_v) + epsilon)
    return (master_new, moment_new, second_new)


def per_device(
    h_in, send_rows, counts, seed_rows, nbr_slot, degree, g_out, weights, master, moment, second
):
    nz, ny, nc, nx = (lax.axis_size(a) for a in ALL)
    peers, block = send_rows.shape[2:]
    vertices, hidden = h_in.shape
    slots = peers * block
    send_ids = send_rows.reshape(peers, block)
    filled = jnp.arange(block, dtype=jnp.int32)[None, :] < counts.reshape(peers)[:, None]
    picks = jnp.where(filled, send_ids, -1).reshape(slots)
    select = (picks[:, None] == jnp.arange(vertices, dtype=jnp.int32)[None, :]).astype(bf16)
    outgoing = dot(select, h_in).astype(bf16)
    received = exchange(outgoing.reshape(peers, block, hidden), OWN).reshape(slots, hidden)

    seed_ids = seed_rows.reshape(-1)
    seeds = seed_ids.shape[0]
    seed_select = (seed_ids[:, None] == jnp.arange(vertices, dtype=jnp.int32)[None, :]).astype(bf16)
    self_rows = dot(seed_select, h_in).astype(bf16)
    self_before = dot(self_rows, weights[:hidden])

    degree = degree.reshape(seeds)
    tallies = tally_slots(nbr_slot.reshape(seeds, -1), degree, slots)
    divisor = degree.astype(f32)[:, None]
    gathered = (dot(tallies, received) / divisor).astype(bf16)
    before = self_before + dot(gathered, weights[hidden:])
    logistic = jax.nn.sigmoid(before)
    h_out = (before * logistic).astype(bf16)
    cotangent = g_out.reshape(seeds, hidden).astype(f32)
    d_before = (cotangent * logistic * (1.0 + before * (1.0 - logistic))).astype(bf16)
    d_scaled = (dot(d_before, weights[hidden:], ((1,), (1,))) / divisor).astype(bf16)
    d_received = dot(tallies, d_scaled, ((0,), (0,))).astype(bf16)
    returned = exchange(d_received.reshape(peers, block, hidden), OWN).reshape(slots, hidden)

    joined = jnp.concatenate([self_rows, gathered], axis=1)
    grad = dot(joined, d_before, ((0,), (0,)))
    shard = grad.shape[0] // (nz * ny * nc * nx)
    grad = grad.reshape(nz * ny, nc, nx * shard, hidden)
    core = lax.axis_index("c")
    mine = lax.dynamic_index_in_dim(grad, core, 1, keepdims=False)
    other = lax.dynamic_index_in_dim(grad, 1 - core, 1, keepdims=False).astype(bf16)
    mine = mine + lax.ppermute(other, "c", [(0, 1), (1, 0)]).astype(f32)
    mine = mine.astype(bf16).reshape(nz * ny, nx, shard, hidden).transpose(1, 0, 2, 3)
    mine = exchange(mine, "x").astype(f32).sum(0).astype(bf16)
    grad_sum = exchange(mine, ("z", "y")).astype(f32).sum(0)
    seed_total = float(seeds * nz * ny * nc * nx)
    master_new, moment_new, second_new = adam_update(grad_sum, master, moment, second, seed_total)
    part = master_new.astype(bf16)
    part = exchange(jnp.broadcast_to(part[None], (nz * ny, shard, hidden)), ("z", "y"))
    part = exchange(jnp.broadcast_to(part[None], (nx,) + part.shape), "x")
    far = lax.ppermute(part, "c", [(0, 1), (1, 0)])
    pair = jnp.where(core == 0, jnp.stack([part, far]), jnp.stack([far, part]))
    weights_new = pair.transpose(2, 0, 1, 3, 4).reshape(weights.shape)

    d_self = dot(d_before, weights[:hidden], ((1,), (1,)))
    d_high = lax.reduce_precision(d_self, 8, 7)
    d_low = (d_self - d_high).astype(bf16)
    d_high = d_high.astype(bf16)
    owner = dot(select, returned, ((0,), (0,)))
    owner = owner + dot(seed_select, d_high, ((0,), (0,))) + dot(seed_select, d_low, ((0,), (0,)))
    parts = exchange(owner.astype(bf16).reshape(nx, vertices // nx, hidden), "x")
    total = parts.astype(f32).sum(0).astype(bf16)
    grad_in = exchange(jnp.broadcast_to(total[None], parts.shape), "x")
    grad_in = grad_in.reshape(vertices, hidden).astype(f32)
    return (h_out.reshape(g_out.shape), grad_in, weights_new, master_new, moment_new, second_new)


def solution(mesh):
    nx = mesh.shape["rep"]
    devices = np.asarray(mesh.devices).reshape(8, 4, 2, nx)
    return jax.shard_map(
        per_device,
        mesh=Mesh(devices, ALL),
        in_specs=(
            P(OWN, None),
            P(OWN, "x", None, None),
            P(OWN, "x", None),
            P(OWN, "x", None),
            P(OWN, "x", None, None),
            P(OWN, "x", None),
            P(OWN, "x", None, None),
            P(),
            P(ALL, None),
            P(ALL, None),
            P(ALL, None),
        ),
        out_specs=(
            P(OWN, "x", None, None),
            P(OWN, None),
            P(),
            P(ALL, None),
            P(ALL, None),
            P(ALL, None),
        ),
        check_vma=False,
    )
```

time: 1570 us -> 387 us (0.25)
  waiting for transfers between devices: 1450 us -> 205 us
  blocking collectives: 0 us -> 84.8 us
  other arithmetic: 38 us -> 13.2 us
    reduce_scatter x1 -> x0, waiting for transfers between devices: 1270 us -> none  [per_device(): lax.psum_scatter(lax.dot_general(joined, d_before, (((0,), (0,)), ((), ()...]
    all_to_all x2 -> x4, waiting for transfers between devices: 93.1 us -> 201 us  [exchange(): return lax.all_to_all(v, axes, split_axis=0, concat_axis=0, tiled=True)]
    all_gather x1 -> x0, waiting for transfers between devices: 91.6 us -> none  [per_device(): weights_new = lax.all_gather(rounded, ('own', 'rep'), axis=0, tiled=True)]
    all_to_all x0 -> x4, blocking collectives: none -> 84.8 us  [exchange(): return lax.all_to_all(v, axes, split_axis=0, concat_axis=0, tiled=True)]
    scatter-add x2 -> x0, other arithmetic: 23.6 us -> none  [the longest x1 19.5 us: per_device(): owner_grad = jnp.zeros(h_in.shape, jnp.float32).at[send_ids.reshape(-1)]....]
    all_to_all x2 -> x4, starting transfers between devices: 21 us -> 32.4 us  [exchange(): return lax.all_to_all(v, axes, split_axis=0, concat_axis=0, tiled=True)]
    dot_general x5 -> x11, matrix products: 22.5 us -> 32.8 us  [dot(): return lax.dot_general(a, b, (dims, ((), ())), preferred_element_type=f32)]
  transfers between devices with their start and end apart: 5 -> 6, of which waited for: 3 -> 5; matrix products, arithmetic and copies ran while one was open for 3% -> 7% of each run, Pallas kernels for 0% -> 0%
where the time goes in v1:
time: 387 us; the launch traced here: 382 us
  waiting for transfers between devices  205 us (53%)
  blocking collectives  84.8 us (22%)
  starting transfers between devices  35.4 us (9%)
  matrix products  32.8 us (8%)
  other arithmetic  13.2 us (3%)
  local copies, waits for them, and re-layouts  9.47 us (2%)
    all_to_all x4, waiting for transfers between devices, exchange(): return lax.all_to_all(v, axes, split_axis=0, concat_axis=0, tiled=True)  201 us
    all_to_all x4, blocking collectives, exchange(): return lax.all_to_all(v, axes, split_axis=0, concat_axis=0, tiled=True)  84.8 us
    dot_general x11, matrix products, dot(): return lax.dot_general(a, b, (dims, ((), ())), preferred_element_type=f32)  32.8 us
    all_to_all x4, starting transfers between devices, exchange(): return lax.all_to_all(v, axes, split_axis=0, concat_axis=0, tiled=True)  32.4 us
  transfers between devices with their start and end apart: 6, of which 5 were waited for; matrix products, arithmetic and copies ran while one was open for 7% of the time, Pallas kernels for 0%

profile of v1, /device:TPU:1, one launch (start us, length us, event | category | flops | bytes accessed | tf_op | source)
XLA Modules:
  0.0 382.0 jit_solution(5128356368222217488)
XLA Ops:
  0.6 0.0 copy-start
  0.6 0.9 copy.24
  1.5 0.1 reshape.140
  1.6 0.7 iota_compare_fusion.17
  2.3 0.1 lt.33
  2.4 0.0 copy-done
  2.4 3.9 %fusion.3 = bf16[2048,1024]{1,0:T(8,128)(2,1)} fusion(bf16[512,1024]{1,0:T(8,128)(2,1)S(1)} %copy-done, s32[2048]{0:T(1024)S(1)} %broadcast_select_fusion), kind=kOutput, calls=%fused_computation.7 | convolution fusion | flops 2150629376 | bytes 5251072 | tf_op jit(solution)/shard_map/dot_general | solution.py:22
  6.4 0.0 copy-start.11
  6.4 0.0 copy-start.10
  6.4 0.0 copy-start.9
  6.4 13.5 %all-to-all-start = ((bf16[64,32,1024]{2,1,0:T(8,128)(2,1)}), bf16[64,32,1024]{2,1,0:T(8,128)(2,1)}, u32[]{:S(2)}, u32[]{:S(2)}) async-start(bf16[64,32,1024]{2,1,0:T(8,128)(2,1)} %bitcast.62), calls=%async_computation | async-start | bytes 8388608 | tf_op jit(solution)/shard_map/all_to_all | solution.py:26
  19.9 0.0 copy-done.11
  20.0 0.0 copy-done.10
  20.0 0.0 copy-done.9
  20.0 0.5 convolution_convert_fusion.1
  20.5 93.8 %all-to-all-done = bf16[64,32,1024]{2,1,0:T(8,128)(2,1)} async-done(((bf16[64,32,1024]{2,1,0:T(8,128)(2,1)}), bf16[64,32,1024]{2,1,0:T(8,128)(2,1)}, u32[]{:S(2)}, u32[]{:S(2)}) %all-to-all-start) | async-done | bytes 4194336 | tf_op jit(solution)/shard_map/all_to_all | solution.py:26
  114.3 6.4 %fusion.27 = bf16[256,1024]{1,0:T(8,128)(2,1)S(1)} fusion(bf16[2048,1024]{1,0:T(8,128)(2,1)} %bitcast.12, f32[256]{0:T(256)S(1)} %bitcast.86, s32[256]{0:T(256)S(1)} %bitcast.72, s32[256]{0:T(256)S(1)} %bitcast.74, s32[256]{0:T(256)S(1)} %bitcast.76, s32[256]{0:T(256)S(1)} %bitcast.78, s32[256]{0:T(256)S(1)} %bitcast.80, s32[256]{0:T(256)S(1)} %bitcast.82, ...), kind=kOutput, calls=%fused_computation.44 | convolution fusion | flops 1091043328 | bytes 4729856 | tf_op jit(solution)/shard_map/dot_general | solution.py:22
  120.7 0.0 copy-done.12
  120.7 0.0 copy-start.13
  120.8 0.7 fusion.18
  121.5 0.3 copy-done.13
  121.8 1.9 fusion.42
  123.7 1.3 fusion.37
  124.9 0.0 copy-done.4
  125.0 0.0 copy-start.2
  125.0 3.2 copy-done.2
  128.2 0.3 fusion.5
  128.5 2.4 collective-permute-start
  131.0 3.9 %collective-permute-done = bf16[32,32,1024]{2,1,0:T(8,128)(2,1)} collective-permute-done((bf16[32,32,1024]{2,1,0:T(8,128)(2,1)S(1)}, bf16[32,32,1024]{2,1,0:T(8,128)(2,1)}, u32[]{:S(2)}, u32[]{:S(2)}) %collective-permute-start) | collective-permute-done | bytes 2097184 | tf_op jit(solution)/shard_map/ppermute | solution.py:88
  134.9 3.6 fusion.4
  138.5 0.2 copy.26
  138.7 29.3 %all_to_all.40 = bf16[4,32,8,1024]{3,2,1,0:T(8,128)(2,1)S(1)} all-to-all(bf16[4,32,8,1024]{3,2,1,0:T(8,128)(2,1)S(1)} %copy.26), channel_id=1, replica_groups=mesh['z'=8,'y'=4,'c'=2,'x'=4] {'x'}, dimensions={0} | all-to-all | bytes 4194304 | tf_op jit(solution)/shard_map/all_to_all | solution.py:26
  168.0 0.4 reduce_sum.34
  168.4 19.3 %all_to_all.41 = bf16[32,8,1024]{2,1,0:T(8,128)(2,1)S(1)} all-to-all(bf16[32,8,1024]{2,1,0:T(8,128)(2,1)S(1)} %reduce_sum.34), channel_id=1, replica_groups=mesh['z'=8,'y'=4,'c'=2,'x'=4] {'z','y'}, dimensions={0} | all-to-all | bytes 1048576 | tf_op jit(solution)/shard_map/all_to_all | solution.py:26
  187.7 0.1 convert_reduce_fusion
  187.7 0.0 copy-done.6
  187.7 0.0 copy-done.7
  187.8 0.0 copy-done.8
  187.8 0.7 fusion.51
  188.5 21.1 %all_to_all.42 = bf16[32,8,1024]{2,1,0:T(8,128)(2,1)S(1)} all-to-all(bf16[32,8,1024]{2,1,0:T(8,128)(2,1)S(1)} %broadcast_in_dim.12), channel_id=1, replica_groups=mesh['z'=8,'y'=4,'c'=2,'x'=4] {'z','y'}, dimensions={0} | all-to-all | bytes 1048576 | tf_op jit(solution)/shard_map/all_to_all | solution.py:26
  209.5 1.6 broadcast_in_dim.13
  211.1 3.7 all-to-all-start.7
  214.9 0.0 copy-done.5
  214.9 8.3 %convolution_convert_fusion = bf16[2048,1024]{1,0:T(8,128)(2,1)} fusion(bf16[256,1024]{1,0:T(8,128)(2,1)S(1)} %copy-done.5, bf16[2048,1024]{1,0:T(8,128)(2,1)} %param.18, f32[256]{0:T(256)S(1)} %bitcast.87, s32[256]{0:T(256)S(1)} %bitcast.73, s32[256]{0:T(256)S(1)} %bitcast.75, s32[256]{0:T(256)S(1)} %bitcast.77, s32[256]{0:T(256)S(1)} %bitcast.79, ...), kind=kOutput, calls=%fused_computation.8 | convolution fusion | flops 1630011392 | bytes 6827008 | tf_op jit(solution)/shard_map/dot_general | solution.py:22
  223.2 14.1 %all-to-all-done.7 = bf16[4,32,8,1024]{3,2,1,0:T(8,128)(2,1)S(1)} async-done(((bf16[4,32,8,1024]{3,2,1,0:T(8,128)(2,1)}), bf16[4,32,8,1024]{3,2,1,0:T(8,128)(2,1)S(1)}, u32[]{:S(2)}, u32[]{:S(2)}) %all-to-all-start.7) | async-done | bytes 2097184 | tf_op jit(solution)/shard_map/all_to_all | solution.py:26
  237.3 11.7 %all-to-all-start.1 = ((bf16[64,32,1024]{2,1,0:T(8,128)(2,1)}), bf16[64,32,1024]{2,1,0:T(8,128)(2,1)}, u32[]{:S(2)}, u32[]{:S(2)}) async-start(bf16[64,32,1024]{2,1,0:T(8,128)(2,1)} %bitcast.63), calls=%async_computation.1 | async-start | bytes 8388608 | tf_op jit(solution)/shard_map/all_to_all | solution.py:26
  249.0 2.5 fusion.20
  251.5 1.9 fusion.44
  253.4 1.6 copy.32
  255.0 0.5 collective-permute-start.1
  255.5 87.9 %all-to-all-done.1 = bf16[64,32,1024]{2,1,0:T(8,128)(2,1)} async-done(((bf16[64,32,1024]{2,1,0:T(8,128)(2,1)}), bf16[64,32,1024]{2,1,0:T(8,128)(2,1)}, u32[]{:S(2)}, u32[]{:S(2)}) %all-to-all-start.1) | async-done | bytes 4194336 | tf_op jit(solution)/shard_map/all_to_all | solution.py:26
  343.4 4.8 %fusion.1 = f32[512,1024]{1,0:T(8,128)S(1)} fusion(bf16[2048,1024]{1,0:T(8,128)(2,1)} %bitcast.17, s32[2048]{0:T(1024)S(1)} %broadcast_select_fusion), kind=kOutput, calls=%fused_computation.5 | convolution fusion | flops 2148532224 | bytes 6299648 | tf_op jit(solution)/shard_map/dot_general | solution.py:22
  348.2 0.0 copy-done.3
  348.2 0.6 add_convert_fusion
  348.8 15.2 %all_to_all.43 = bf16[4,128,1024]{2,1,0:T(8,128)(2,1)S(1)} all-to-all(bf16[4,128,1024]{2,1,0:T(8,128)(2,1)S(1)} %bitcast.65), channel_id=1, replica_groups=mesh['z'=8,'y'=4,'c'=2,'x'=4] {'x'}, dimensions={0} | all-to-all | bytes 2097152 | tf_op jit(solution)/shard_map/all_to_all | solution.py:26
  364.0 0.2 reduce_sum.33
  364.2 1.1 broadcast_in_dim.11
  365.3 3.5 all-to-all-start.3
  368.8 0.0 collective-permute-done.1
  368.9 0.0 copy-start.1
  368.9 5.9 %maximum_select_fusion = bf16[2,4,32,8,1024]{4,3,1,0,2:T(8,128)(2,1)} fusion(bf16[1,4,32,8,1024]{4,3,1,0,2:T(8,128)(2,1)} %bitcast.26, bf16[1,4,32,8,1024]{4,3,1,0,2:T(8,128)(2,1)} %bitcast.59, pred[]{:T(512)S(6)} %eq.190), kind=kLoop, calls=%fused_computation | loop fusion | flops 6291456 | bytes 8388609 | tf_op jit(solution)/shard_map/jit(_where)/select_n | solution.py:98
  374.7 5.6 %all-to-all-done.3 = bf16[4,128,1024]{2,1,0:T(8,128)(2,1)S(1)} async-done(((bf16[4,128,1024]{2,1,0:T(8,128)(2,1)}), bf16[4,128,1024]{2,1,0:T(8,128)(2,1)S(1)}, u32[]{:S(2)}, u32[]{:S(2)}) %all-to-all-start.3) | async-done | bytes 1048608 | tf_op jit(solution)/shard_map/all_to_all | solution.py:26
  380.4 1.6 bitcast_convert_fusion.1
  382.0 0.0 copy-done.1
  (12 shorter events, 0.1 us)
Async XLA Ops:
  0.6 1.8 copy-start
  6.4 13.5 %copy-start.11 = (s32[1,1,256]{2,1,0:T(1,128)S(1)}, s32[1,1,256]{2,1,0:T(1,128)}, u32[]{:S(2)}) copy-start(s32[1,1,256]{2,1,0:T(1,128)} %param.16) | copy-start | bytes 3076
  6.4 13.6 %copy-start.10 = (s32[1,1,256,8]{2,3,1,0:T(8,128)S(1)}, s32[1,1,256,8]{2,3,1,0:T(8,128)}, u32[]{:S(2)}) copy-start(s32[1,1,256,8]{2,3,1,0:T(8,128)} %param.15) | copy-start | bytes 24580
  6.4 13.6 %copy-start.9 = (s32[1,1,256]{2,1,0:T(1,128)S(1)}, s32[1,1,256]{2,1,0:T(1,128)}, u32[]{:S(2)}) copy-start(s32[1,1,256]{2,1,0:T(1,128)} %param.14) | copy-start | bytes 3076
  6.4 107.9 %all-to-all-start = ((bf16[64,32,1024]{2,1,0:T(8,128)(2,1)}), bf16[64,32,1024]{2,1,0:T(8,128)(2,1)}, u32[]{:S(2)}, u32[]{:S(2)}) async-start(bf16[64,32,1024]{2,1,0:T(8,128)(2,1)} %bitcast.62), calls=%async_computation | async-start | bytes 8388608 | tf_op jit(solution)/shard_map/all_to_all | solution.py:26
  114.3 6.4 %copy-start.12 = (bf16[2048,1024]{1,0:T(8,128)(2,1)S(1)}, bf16[2048,1024]{1,0:T(8,128)(2,1)}, u32[]{:S(2)}) copy-start(bf16[2048,1024]{1,0:T(8,128)(2,1)} %param.18) | copy-start | bytes 12582916
  120.7 1.0 copy-start.13
  123.7 1.3 copy-start.4
  125.0 3.2 copy-start.2
  128.5 6.4 %collective-permute-start = (bf16[32,32,1024]{2,1,0:T(8,128)(2,1)S(1)}, bf16[32,32,1024]{2,1,0:T(8,128)(2,1)}, u32[]{:S(2)}, u32[]{:S(2)}) collective-permute-start(bf16[32,32,1024]{2,1,0:T(8,128)(2,1)S(1)} %fusion.5), channel_id=1, source_target_pairs={{0,4},{4,0},{1,5},{5,1},{2,6},{6,2},{3,7},{7,3},{8,12},{12,8},{9,1... | collective-permute-start | bytes 6291464 | tf_op jit(solution)/shard_map/ppermute | solution.py:88
  168.0 19.8 %copy-start.6 = (f32[8,1024]{1,0:T(8,128)S(1)}, f32[8,1024]{1,0:T(8,128)}, u32[]{:S(2)}) copy-start(f32[8,1024]{1,0:T(8,128)} %param.19) | copy-start | bytes 98308
  168.0 19.8 %copy-start.7 = (f32[8,1024]{1,0:T(8,128)S(1)}, f32[8,1024]{1,0:T(8,128)}, u32[]{:S(2)}) copy-start(f32[8,1024]{1,0:T(8,128)} %param.20) | copy-start | bytes 98308
  168.0 19.8 %copy-start.8 = (f32[8,1024]{1,0:T(8,128)S(1)}, f32[8,1024]{1,0:T(8,128)}, u32[]{:S(2)}) copy-start(f32[8,1024]{1,0:T(8,128)} %param.21) | copy-start | bytes 98308
  211.1 3.8 copy-start.5
  211.1 26.2 %all-to-all-start.7 = ((bf16[4,32,8,1024]{3,2,1,0:T(8,128)(2,1)}), bf16[4,32,8,1024]{3,2,1,0:T(8,128)(2,1)S(1)}, u32[]{:S(2)}, u32[]{:S(2)}) async-start(bf16[4,32,8,1024]{3,2,1,0:T(8,128)(2,1)} %broadcast_in_dim.13), calls=%async_computation.7 | async-start | bytes 4194304 | tf_op jit(solution)/shard_map/all_to_all | solution.py:26
  237.3 106.1 %all-to-all-start.1 = ((bf16[64,32,1024]{2,1,0:T(8,128)(2,1)}), bf16[64,32,1024]{2,1,0:T(8,128)(2,1)}, u32[]{:S(2)}, u32[]{:S(2)}) async-start(bf16[64,32,1024]{2,1,0:T(8,128)(2,1)} %bitcast.63), calls=%async_computation.1 | async-start | bytes 8388608 | tf_op jit(solution)/shard_map/all_to_all | solution.py:26
  255.0 113.8 %collective-permute-start.1 = (bf16[4,32,8,1024]{3,2,0,1:T(8,128)(2,1)}, bf16[4,32,8,1024]{3,2,0,1:T(8,128)(2,1)}, u32[]{:S(2)}, u32[]{:S(2)}) collective-permute-start(bf16[4,32,8,1024]{3,2,0,1:T(8,128)(2,1)} %copy.32), channel_id=1, source_target_pairs={{0,4},{4,0},{1,5},{5,1},{2,6},{6,2},{3,7},{7,3},{8,12},{12,8},{9,1... | collective-permute-start | bytes 6291464 | tf_op jit(solution)/shard_map/ppermute | solution.py:97
  343.4 4.8 %copy-start.3 = (f32[512,1024]{1,0:T(8,128)S(1)}, f32[512,1024]{1,0:T(8,128)}, u32[]{:S(2)}) copy-start(f32[512,1024]{1,0:T(8,128)} %fusion.44) | copy-start | bytes 6291460
  365.3 15.0 %all-to-all-start.3 = ((bf16[4,128,1024]{2,1,0:T(8,128)(2,1)}), bf16[4,128,1024]{2,1,0:T(8,128)(2,1)S(1)}, u32[]{:S(2)}, u32[]{:S(2)}) async-start(bf16[4,128,1024]{2,1,0:T(8,128)(2,1)} %broadcast_in_dim.11), calls=%async_computation.3 | async-start | bytes 2097152 | tf_op jit(solution)/shard_map/all_to_all | solution.py:26
  368.9 13.1 %copy-start.1 = (bf16[512,1024]{1,0:T(8,128)(2,1)S(1)}, bf16[512,1024]{1,0:T(8,128)(2,1)}, u32[]{:S(2)}) copy-start(bf16[512,1024]{1,0:T(8,128)(2,1)} %param.11) | copy-start | bytes 3145732
